TPU v7x, 512 devices: a whole 4x4x16 slice. The times are simulated.
512 devices in a mesh: chan: 32 (over z, y_hi), win: 16 (over y_lo, x, core).
Axes of the slice: x: 4, y: 4 (y_hi: 2, y_lo: 2; y = y_hi * 2 + y_lo), z: 16, core: 2. Of those that a mesh axis runs over, the one named last changes fastest.
Arguments:
- spectra: bfloat16 [32, 10240, 2, 512], P('win', 'chan')
- counts: int32 [32], P('chan'), may hold values from 160 to 320, as said below
- partner: int32 [1, 32], replicated, may hold values from 0 to 31, as said below
Outputs:
- corr: float32 [32, 1, 16, 160, 320], P('chan', None, None, 'win')
Inputs may be any that keep to these rules, and one draw needn't show every extreme that they name: `counts`: every block has at least 160 live channels and some block has all 320. partner[q, b] = b XOR t_q for distinct nonzero round numbers t_q, so every round pairs the blocks among themselves.
All inputs are finite; a program needn't handle non-finite values.
Results may differ from a plain program's by a relative error of at most 0.0049.
Values may be sent and summed in bfloat16 or wider, within the bound.
A program may use at most 64 MiB of HBM per device.

v0:
```python
import math

import jax
import jax.numpy as jnp
from jax import lax
from jax.sharding import PartitionSpec as P

LAGS = 16
SRC = 160


def from_partner(value, axis, stride):
    return lax.ppermute(value, axis, [(i, i ^ 1 << stride) for i in range(lax.axis_size(axis))])


def whiten_local(spectra, count):
    values = spectra.astype(jnp.float32)
    block_size = spectra.shape[1]
    freqs = spectra.shape[3]
    valid = (jnp.arange(block_size, dtype=jnp.int32) < count).astype(jnp.float32)
    freq = jnp.arange(freqs, dtype=jnp.float32)
    taper = 0.75 - 0.25 * jnp.cos(2.0 * math.pi * (freq + 0.5) / freqs)
    power = jnp.mean(values * values, axis=(2, 3))
    scale = valid[None, :] / jnp.sqrt(power + 1e-05)
    return (values * taper * scale[:, :, None, None]).astype(jnp.bfloat16)


def lag_table(freqs, lags):
    freq = jnp.arange(freqs, dtype=jnp.float32) + freqs // 4
    delay = jnp.arange(lags, dtype=jnp.float32) - lags // 2
    phase = 2.0 * math.pi * freq[:, None] * delay[None, :] / (4.0 * freqs)
    norm = 1.0 / math.sqrt(2.0 * freqs)
    return jnp.stack([jnp.cos(phase), -jnp.sin(phase)]) * norm


def blended_sources(sources, table):
    src = sources.astype(jnp.float32)
    first = src[:, :, 0][:, :, None, :]
    second = src[:, :, 1][:, :, None, :]
    cos_part = table[0].T[None, None]
    sin_part = table[1].T[None, None]
    real_mix = first * cos_part + second * sin_part
    imag_mix = second * cos_part - first * sin_part
    return jnp.stack([real_mix, imag_mix], axis=3).astype(jnp.bfloat16)


def pair_terms(sources, receiver_blocks, table):
    wins, count, two, freqs = sources.shape
    lags = table.shape[2]
    group = math.gcd(count, 32)
    flat_recv = receiver_blocks.reshape(wins, receiver_blocks.shape[1], two * freqs)
    grouped = jnp.moveaxis(sources.reshape(wins, count // group, group, two, freqs), 1, 0)

    def one_group(piece):
        mixed_spectra = blended_sources(piece, table).reshape(wins, group * lags, two * freqs)
        out = jnp.einsum(
            "wmx,wrx->mr", mixed_spectra, flat_recv, preferred_element_type=jnp.float32
        )
        return out.reshape(group, lags, receiver_blocks.shape[1])

    terms = lax.map(one_group, grouped).reshape(count, lags, receiver_blocks.shape[1])
    return jnp.transpose(terms, (1, 0, 2))


def route_blocks(values, round_flags, levels):
    for level in range(levels):
        moved = from_partner(values, "chan", level)
        values = jnp.where((round_flags >> level) % 2 == 1, moved, values)
    return values


def body(spectra, counts, partner):
    white = whiten_local(spectra, counts[0])
    table = lag_table(spectra.shape[3], LAGS)
    levels = lax.axis_size("chan").bit_length() - 1
    windows = spectra.shape[0] * lax.axis_size("win")
    round_flags = partner[0, 0]
    receiver_blocks = route_blocks(white, round_flags, levels)
    terms = pair_terms(white[:, :SRC], receiver_blocks, table)
    stacked = lax.psum_scatter(terms, "win", scatter_dimension=1, tiled=True)
    pair_outputs = [stacked]
    return (jnp.stack(pair_outputs, axis=0) / math.sqrt(windows))[None]


def solution(mesh):
    return jax.shard_map(
        body,
        mesh=mesh,
        in_specs=(P("win", "chan", None, None), P("chan"), P()),
        out_specs=P("chan", None, None, "win", None),
        check_vma=False,
    )
```

profile of v0, /device:TPU:32, one launch (start us, length us, event | category | flops | bytes accessed | tf_op | source)
XLA Modules:
  0.0 574.5 jit_solution(2840642638779838650)
XLA Ops:
  6.5 0.0 reduce-scatter.2.cloned.1.call-start
  6.6 1.7 fusion.11
  9.0 0.0 copy-done
  9.0 0.3 fusion.10
  9.4 0.0 copy-start.1
  9.4 5.1 collective-permute-start
  14.6 0.0 copy-done.1
  14.6 28.8 %collective-permute-done = bf16[2,320,2,512]{3,1,2,0:T(8,128)(2,1)} collective-permute-done((bf16[2,320,2,512]{3,1,2,0:T(8,128)(2,1)S(1)}, bf16[2,320,2,512]{3,1,2,0:T(8,128)(2,1)}, u32[]{:S(2)}, u32[]{:S(2)}) %collective-permute-start) | collective-permute-done | bytes 1310752 | tf_op jit(solution)/shard_map/ppermute | solution.py:13
  43.4 1.8 broadcast_select_fusion
  45.2 2.0 collective-permute-start.1
  47.3 29.6 %collective-permute-done.1 = bf16[2,320,2,512]{3,1,2,0:T(8,128)(2,1)} collective-permute-done((bf16[2,320,2,512]{3,1,2,0:T(8,128)(2,1)S(1)}, bf16[2,320,2,512]{3,1,2,0:T(8,128)(2,1)}, u32[]{:S(2)}, u32[]{:S(2)}) %collective-permute-start.1) | collective-permute-done | bytes 1310752 | tf_op jit(solution)/shard_map/ppermute | solution.py:13
  76.9 0.1 broadcast_select_fusion.1
  77.0 5.2 collective-permute-start.2
  82.2 54.2 %collective-permute-done.2 = bf16[2,320,2,512]{3,1,2,0:T(8,128)(2,1)} collective-permute-done((bf16[2,320,2,512]{3,1,2,0:T(8,128)(2,1)S(1)}, bf16[2,320,2,512]{3,1,2,0:T(8,128)(2,1)}, u32[]{:S(2)}, u32[]{:S(2)}) %collective-permute-start.2) | collective-permute-done | bytes 1310752 | tf_op jit(solution)/shard_map/ppermute | solution.py:13
  136.4 0.1 broadcast_select_fusion.2
  136.6 9.1 %collective-permute-start.3 = (bf16[2,320,2,512]{3,1,2,0:T(8,128)(2,1)S(1)}, bf16[2,320,2,512]{3,1,2,0:T(8,128)(2,1)}, u32[]{:S(2)}, u32[]{:S(2)}) collective-permute-start(bf16[2,320,2,512]{3,1,2,0:T(8,128)(2,1)S(1)} %broadcast_select_fusion.2), channel_id=1, source_target_pairs={{0,128},{16,144},{32,160},{48,176},{64,192},{80,208},{96,224},{112... | collective-permute-start | bytes 3932168 | tf_op jit(solution)/shard_map/ppermute | solution.py:13
  145.7 83.0 %collective-permute-done.3 = bf16[2,320,2,512]{3,1,2,0:T(8,128)(2,1)} collective-permute-done((bf16[2,320,2,512]{3,1,2,0:T(8,128)(2,1)S(1)}, bf16[2,320,2,512]{3,1,2,0:T(8,128)(2,1)}, u32[]{:S(2)}, u32[]{:S(2)}) %collective-permute-start.3) | collective-permute-done | bytes 1310752 | tf_op jit(solution)/shard_map/ppermute | solution.py:13
  228.8 1.5 broadcast_select_fusion.3
  230.2 13.3 %collective-permute-start.4 = (bf16[2,320,2,512]{3,1,2,0:T(8,128)(2,1)S(1)}, bf16[2,320,2,512]{3,1,2,0:T(8,128)(2,1)S(1)}, u32[]{:S(2)}, u32[]{:S(2)}) collective-permute-start(bf16[2,320,2,512]{3,1,2,0:T(8,128)(2,1)S(1)} %broadcast_select_fusion.3), channel_id=1, source_target_pairs={{0,256},{16,272},{32,288},{48,304},{64,320},{80,336},{96,352},{112... | collective-permute-start | bytes 3932168 | tf_op jit(solution)/shard_map/ppermute | solution.py:13
  243.6 1.1 slice.22
  244.7 0.2 fusion.12
  245.0 77.9 %collective-permute-done.4 = bf16[2,320,2,512]{3,1,2,0:T(8,128)(2,1)S(1)} collective-permute-done((bf16[2,320,2,512]{3,1,2,0:T(8,128)(2,1)S(1)}, bf16[2,320,2,512]{3,1,2,0:T(8,128)(2,1)S(1)}, u32[]{:S(2)}, u32[]{:S(2)}) %collective-permute-start.4) | collective-permute-done | bytes 1310752 | tf_op jit(solution)/shard_map/ppermute | solution.py:13
  322.9 0.1 select_bitcast_fusion
  323.0 1.3 copy.12
  324.3 81.0 %while.10 = (s32[]{:T(128)}, f32[5,32,16,320]{3,2,1,0:T(8,128)}, bf16[5,2,32,2,512]{4,2,0,3,1:T(8,128)(2,1)S(1)}, f32[2,512,16]{1,2,0:T(8,128)S(1)}, bf16[2,320,1024]{2,1,0:T(8,128)(2,1)}, /*index=5*/s32[]{:T(128)}) while((s32[]{:T(128)}, f32[5,32,16,320]{3,2,1,0:T(8,128)}, bf16[5,2,32,2,512]{4,2,0,3,1:T(8,128)(2,1)S(1)}, ...), condition=%wide.region_2.3_spmd, body=%wide.region_1.2_spmd.sunk | while | flops 679542784 | bytes 16056905 | solution.py:61
  324.4 4.4 add_convert_fusion.2
  328.8 4.8 pad_maximum_fusion.2
  333.6 2.7 convert_element_type.43
  336.4 4.1 fusion.22
  340.5 4.4 add_convert_fusion.2
  345.0 4.8 pad_maximum_fusion.2
  349.8 2.7 convert_element_type.43
  352.6 4.1 fusion.22
  356.8 4.4 add_convert_fusion.2
  361.2 4.8 pad_maximum_fusion.2
  366.0 2.7 convert_element_type.43
  368.8 4.1 fusion.22
  372.9 4.4 add_convert_fusion.2
  377.4 4.8 pad_maximum_fusion.2
  382.2 2.7 convert_element_type.43
  385.0 4.1 fusion.22
  389.1 4.4 add_convert_fusion.2
  393.6 4.8 pad_maximum_fusion.2
  398.4 2.7 convert_element_type.43
  401.1 4.1 fusion.22
  405.2 0.0 reduce-scatter.2.cloned.1.call-update
  405.3 160.7 %reduce-scatter.2.cloned.1.call-done = f32[16,10,320]{2,0,1:T(8,128)} async-done(((f32[16,160,320]{2,0,1:T(8,128)}), f32[16,10,320]{2,0,1:T(8,128)}) %reduce-scatter.2.cloned.1.call-update) | async-done | bytes 204816 | tf_op jit(solution)/shard_map/reduce_scatter | solution.py:80
  566.0 1.7 multiply_bitcast_fusion
  (25 shorter events, 0.3 us)
Async XLA Ops:
  6.5 2.5 copy-start
  6.5 8.0 %copy-start.2 = (s32[1,32]{1,0:T(1,128)S(1)}, s32[1,32]{1,0:T(1,128)}, u32[]{:S(2)}) copy-start(s32[1,32]{1,0:T(1,128)} %param.7) | copy-start | bytes 388
  6.5 559.4 %reduce-scatter.2.cloned.1.call-start = ((), (), s32[]{:S(2)}) async-start(), calls=%async_computation.1 | async-start | bytes 4177920 | tf_op jit(solution)/shard_map/reduce_scatter | solution.py:80
  9.4 5.2 copy-start.1
  9.4 34.0 %collective-permute-start = (bf16[2,320,2,512]{3,1,2,0:T(8,128)(2,1)S(1)}, bf16[2,320,2,512]{3,1,2,0:T(8,128)(2,1)}, u32[]{:S(2)}, u32[]{:S(2)}) collective-permute-start(bf16[2,320,2,512]{3,1,2,0:T(8,128)(2,1)S(1)} %fusion.10), channel_id=1, source_target_pairs={{0,16},{16,0},{32,48},{48,32},{64,80},{80,64},{96,112},{112,96},{1... | collective-permute-start | bytes 3932168 | tf_op jit(solution)/shard_map/ppermute | solution.py:13
  45.2 31.6 %collective-permute-start.1 = (bf16[2,320,2,512]{3,1,2,0:T(8,128)(2,1)S(1)}, bf16[2,320,2,512]{3,1,2,0:T(8,128)(2,1)}, u32[]{:S(2)}, u32[]{:S(2)}) collective-permute-start(bf16[2,320,2,512]{3,1,2,0:T(8,128)(2,1)S(1)} %broadcast_select_fusion), channel_id=1, source_target_pairs={{0,32},{16,48},{32,0},{48,16},{64,96},{80,112},{96,64},{112,80},{1... | collective-permute-start | bytes 3932168 | tf_op jit(solution)/shard_map/ppermute | solution.py:13
  77.0 59.4 %collective-permute-start.2 = (bf16[2,320,2,512]{3,1,2,0:T(8,128)(2,1)S(1)}, bf16[2,320,2,512]{3,1,2,0:T(8,128)(2,1)}, u32[]{:S(2)}, u32[]{:S(2)}) collective-permute-start(bf16[2,320,2,512]{3,1,2,0:T(8,128)(2,1)S(1)} %broadcast_select_fusion.1), channel_id=1, source_target_pairs={{0,64},{16,80},{32,96},{48,112},{64,0},{80,16},{96,32},{112,48},{1... | collective-permute-start | bytes 3932168 | tf_op jit(solution)/shard_map/ppermute | solution.py:13
  136.6 92.2 %collective-permute-start.3 = (bf16[2,320,2,512]{3,1,2,0:T(8,128)(2,1)S(1)}, bf16[2,320,2,512]{3,1,2,0:T(8,128)(2,1)}, u32[]{:S(2)}, u32[]{:S(2)}) collective-permute-start(bf16[2,320,2,512]{3,1,2,0:T(8,128)(2,1)S(1)} %broadcast_select_fusion.2), channel_id=1, source_target_pairs={{0,128},{16,144},{32,160},{48,176},{64,192},{80,208},{96,224},{112... | collective-permute-start | bytes 3932168 | tf_op jit(solution)/shard_map/ppermute | solution.py:13
  230.2 92.7 %collective-permute-start.4 = (bf16[2,320,2,512]{3,1,2,0:T(8,128)(2,1)S(1)}, bf16[2,320,2,512]{3,1,2,0:T(8,128)(2,1)S(1)}, u32[]{:S(2)}, u32[]{:S(2)}) collective-permute-start(bf16[2,320,2,512]{3,1,2,0:T(8,128)(2,1)S(1)} %broadcast_select_fusion.3), channel_id=1, source_target_pairs={{0,256},{16,272},{32,288},{48,304},{64,320},{80,336},{96,352},{112... | collective-permute-start | bytes 3932168 | tf_op jit(solution)/shard_map/ppermute | solution.py:13
Sparse Core Ops, SparseCore 0:
  405.4 160.5 reduce-scatter.1
where the time goes:
time: 575 us; the launch traced here: 574 us
  waiting for transfers between devices  434 us (75%)
  other arithmetic  54.2 us (9%)
  starting transfers between devices  34.6 us (6%)
  matrix products  20.5 us (4%)
  local copies, waits for them, and re-layouts  16.2 us (3%)
  between operations  14.4 us (3%)
    ppermute x5, waiting for transfers between devices, from_partner(): lax.ppermute(value, axis, [(i, i ^ 1 << stride) for i in range(lax.axis_s...  274 us
    reduce_scatter x1, waiting for transfers between devices, body(): stacked = lax.psum_scatter(terms, 'win', scatter_dimension=1, tiled=True)  161 us
    ppermute x5, starting transfers between devices, from_partner(): lax.ppermute(value, axis, [(i, i ^ 1 << stride) for i in range(lax.axis_s...  34.6 us
    another operation x5, other arithmetic, blended_sources(): return jnp.stack([real_mix, imag_mix], axis=3).astype(jnp.bfloat16)  24.2 us
    another operation x5, other arithmetic  22.2 us
    dot_general x5, matrix products, one_group(): jnp.einsum('wmx,wrx->mr', mixed_spectra, flat_recv, preferred_element_typ...  20.5 us
    convert_element_type x5, local copies, waits for them, and re-layouts, blended_sources(): return jnp.stack([real_mix, imag_mix], axis=3).astype(jnp.bfloat16)  13.6 us
  transfers between devices with their start and end apart: 6, of which 6 were waited for; matrix products, arithmetic and copies ran while one was open for 0% of the time, Pallas kernels for 0%

commit v1 on v0

v1 whole, which is shorter than its diff:
```python
import functools
import math

import jax
import jax.numpy as jnp
from jax import lax
from jax.experimental import pallas as pl
from jax.experimental.pallas import tpu as pltpu
from jax.sharding import PartitionSpec as P

LAGS = 16
SRC = 160
MESH = pl.DeviceIdType.MESH


def whiten_rows(spectra, count):
    values = spectra.astype(jnp.float32)
    wins, block_size, two, freqs = spectra.shape
    valid = (jnp.arange(block_size, dtype=jnp.int32) < count).astype(jnp.float32)
    freq = jnp.arange(freqs, dtype=jnp.float32)
    taper = 0.75 - 0.25 * jnp.cos(2.0 * math.pi * (freq + 0.5) / freqs)
    power = jnp.mean(values * values, axis=(2, 3))
    scale = valid[None, :] / jnp.sqrt(power + 1e-05)
    white = (values * taper * scale[:, :, None, None]).astype(jnp.bfloat16)
    return jnp.swapaxes(white, 0, 1).reshape(block_size, wins * two * freqs)


def lag_table(freqs, lags):
    freq = jnp.arange(freqs, dtype=jnp.float32) + freqs // 4
    delay = jnp.arange(lags, dtype=jnp.float32) - lags // 2
    phase = 2.0 * math.pi * freq[None, :] * delay[:, None] / (4.0 * freqs)
    norm = 1.0 / math.sqrt(2.0 * freqs)
    return jnp.cos(phase) * norm, -jnp.sin(phase) * norm


def correlate_kernel(
    scale, src_ref, rec_ref, cos_ref, sin_ref, out_ref,
    src32, mixed, send1, recv1, send2, recv2, sem_s1, sem_r1, sem_s2, sem_r2,
):
    chan = lax.axis_index("chan")
    win = lax.axis_index("win")
    y, x, core = win // 8, lax.rem(win // 2, 4), lax.rem(win, 2)
    sibling = win + 1 - 2 * core
    per = SRC // 16
    rows = per * LAGS
    freqs = cos_ref.shape[1]
    wins = src_ref.shape[1] // (2 * freqs)

    def place(d):
        return lax.rem(y + d // 4, 2) * 8 + lax.rem(x + lax.rem(d, 4), 4) * 2

    barrier = pltpu.get_barrier_semaphore()
    pl.semaphore_signal(barrier, inc=1, device_id=(chan, sibling), device_id_type=MESH)
    for d in range(1, 8):
        pl.semaphore_signal(barrier, inc=1, device_id=(chan, place(d) + core), device_id_type=MESH)
    pl.semaphore_wait(barrier, 8)

    src32[...] = src_ref[...].astype(jnp.float32)

    def block(dest):
        total = None
        for w in range(wins):
            for i in range(per):
                s = dest * per + i
                first = src32[pl.ds(s, 1), 2 * w * freqs : (2 * w + 1) * freqs]
                second = src32[pl.ds(s, 1), (2 * w + 1) * freqs : (2 * w + 2) * freqs]
                cos, sin = cos_ref[...], sin_ref[...]
                mixed[w, i * LAGS : (i + 1) * LAGS, :freqs] = (first * cos + second * sin).astype(jnp.bfloat16)
                mixed[w, i * LAGS : (i + 1) * LAGS, freqs:] = (second * cos - first * sin).astype(jnp.bfloat16)
            term = lax.dot_general(
                mixed[w], rec_ref[:, 2 * w * freqs : (2 * w + 2) * freqs],
                (((1,), (1,)), ((), ())), preferred_element_type=jnp.float32,
            )
            total = term if total is None else total + term
        return total

    def copy1(d):
        return pltpu.make_async_remote_copy(
            src_ref=send1.at[d], dst_ref=recv1.at[d], send_sem=sem_s1.at[d], recv_sem=sem_r1.at[d],
            device_id=(chan, sibling), device_id_type=MESH,
        )

    def copy2(d):
        return pltpu.make_async_remote_copy(
            src_ref=send2.at[d], dst_ref=recv2.at[d], send_sem=sem_s2.at[d], recv_sem=sem_r2.at[d],
            device_id=(chan, place(d) + core), device_id_type=MESH,
        )

    @pl.loop(0, 8)
    def _(n):
        d = 7 - n
        send1[d] = block(place(d) + 1 - core).astype(jnp.bfloat16)
        copy1(d).start()

    @pl.loop(0, 7)
    def _(n):
        d = 7 - n
        part = block(place(d) + core)
        copy1(d).wait_recv()
        send2[d] = (part + recv1[d].astype(jnp.float32)).astype(jnp.bfloat16)
        copy2(d).start()

    total = block(win)
    copy1(0).wait_recv()
    total = total + recv1[0].astype(jnp.float32)
    for d in range(1, 8):
        copy2(d).wait_recv()
        total = total + recv2[d].astype(jnp.float32)
    out_ref[...] = (total * scale).astype(out_ref.dtype)
    for d in range(8):
        copy1(d).wait_send()
    for d in range(1, 8):
        copy2(d).wait_send()


def correlate(sources, receivers, cos, sin, scale):
    count, width = receivers.shape
    rows = SRC // 16 * LAGS
    blocks = pltpu.VMEM((8, rows, count), jnp.bfloat16)
    whole = pl.BlockSpec(memory_space=pltpu.VMEM)
    return pl.pallas_call(
        functools.partial(correlate_kernel, scale),
        out_shape=jax.ShapeDtypeStruct((rows, count), jnp.bfloat16),
        in_specs=[whole] * 4,
        out_specs=whole,
        scratch_shapes=[
            pltpu.VMEM((SRC, width), jnp.float32),
            pltpu.VMEM((width // (2 * cos.shape[1]), rows, 2 * cos.shape[1]), jnp.bfloat16),
            blocks, blocks, blocks, blocks,
            pltpu.SemaphoreType.DMA((8,)), pltpu.SemaphoreType.DMA((8,)),
            pltpu.SemaphoreType.DMA((8,)), pltpu.SemaphoreType.DMA((8,)),
        ],
        compiler_params=pltpu.CompilerParams(
            collective_id=0, has_side_effects=True, vmem_limit_bytes=32 * 1024 * 1024
        ),
        cost_estimate=pl.CostEstimate(
            flops=2 * SRC * LAGS * count * width, bytes_accessed=4 * count * width, transcendentals=0
        ),
        name="correlate",
    )(sources, receivers, cos, sin)


def exchange(values, flags, size):
    branches = [
        functools.partial(lax.ppermute, axis_name="chan", perm=[(i, i ^ t) for i in range(size)])
        for t in range(1, size)
    ]
    return lax.switch(flags - 1, branches, values)


def body(spectra, counts, partner):
    white = whiten_rows(spectra, counts[0])
    cos, sin = lag_table(spectra.shape[3], LAGS)
    size = lax.axis_size("chan")
    windows = spectra.shape[0] * lax.axis_size("win")
    flags = partner[0, 0]
    sources = exchange(white[:SRC], flags, size)
    block = correlate(sources, white, cos, sin, 1.0 / math.sqrt(windows))
    block = exchange(block, flags, size)
    out = jnp.swapaxes(block.astype(jnp.float32).reshape(SRC // 16, LAGS, white.shape[0]), 0, 1)
    return out[None, None]


def solution(mesh):
    return jax.shard_map(
        body,
        mesh=mesh,
        in_specs=(P("win", "chan", None, None), P("chan"), P()),
        out_specs=P("chan", None, None, "win", None),
        check_vma=False,
    )
```

time: 575 us -> 112 us (0.19)
  the two profiles are of different devices: /device:TPU:32 before, /device:TPU:34 now
where the time goes in v1:
time: 112 us
  waiting for transfers between devices  67.5 us (60%)
  Pallas kernels  23.8 us (21%)
  starting transfers between devices  9.67 us (9%)
  other arithmetic  7.02 us (6%)
  local copies, waits for them, and re-layouts  3.31 us (3%)
    ppermute x2, waiting for transfers between devices, exchange(): return lax.switch(flags - 1, branches, values)  67.5 us
    pallas_call x1, Pallas kernels, correlate(): pl.pallas_call(functools.partial(correlate_kernel, scale), out_shape=jax....  23.8 us
    ppermute x2, starting transfers between devices, exchange(): return lax.switch(flags - 1, branches, values)  9.67 us
    reduce_sum x1, other arithmetic, whiten_rows(): power = jnp.mean(values * values, axis=(2, 3))  3.49 us
  transfers between devices with their start and end apart: 2, of which 2 were waited for; matrix products, arithmetic and copies ran while one was open for 0% of the time, Pallas kernels for 0%

profile of v1, /device:TPU:34, one launch (start us, length us, event | category | flops | bytes accessed | tf_op | source)
XLA Modules:
  0.0 112.2 jit_solution(14294554866515922387)
XLA Ops:
  0.0 0.0 copy-start
  0.0 3.5 %fusion.2 = f32[2,320]{1,0:T(2,128)S(1)} fusion(bf16[2,320,2,512]{3,2,1,0:T(2,128)(2,1)} %param.65), kind=kLoop, calls=%fused_computation.4 | loop fusion | flops 1965440 | bytes 1313280 | tf_op jit(solution)/shard_map/reduce_sum | solution.py:22
  4.2 0.0 copy-done
  4.2 1.6 %fusion.3 = bf16[320,2,2,512]{3,2,0,1:T(2,128)(2,1)S(1)} fusion(bf16[2,320,2,512]{3,2,1,0:T(2,128)(2,1)S(1)} %copy-done, f32[2,320]{1,0:T(2,128)S(1)} %rsqrt_multiply_fusion, f32[512]{0:T(512)S(1)} %multiply_subtract_fusion), kind=kLoop, calls=%fused_computation.5 | loop fusion | flops 2621440 | bytes 2626048 | tf_op jit(solution)/shard_map/transpose | solution.py:25
  5.9 0.5 slice.105
  6.3 0.0 copy-start.1
  6.3 0.5 copy.4
  6.8 0.5 slice.104
  7.3 0.0 copy-done.1
  7.4 64.7 %conditional.2 = (bf16[160,2048]{1,0:T(8,128)(2,1)}) conditional(s32[]{:T(128)} %bitcast, bf16[160,2048]{1,0:T(8,128)(2,1)S(1)} %slice.104, bf16[160,2048]{1,0:T(8,128)(2,1)S(1)} %slice.104, bf16[160,2048]{1,0:T(8,128)(2,1)S(1)} %slice.104, bf16[160,2048]{1,0:T(8,128)(2,1)S(1)} %slice.104, ...), branch_computations={%region_1.0_spmd, %region_2.0_spmd, %region_3.0_spmd, %region_4.0_... | conditional | bytes 2621488 | solution.py:148
  7.4 7.7 %collective-permute-start.9 = (bf16[160,2048]{1,0:T(8,128)(2,1)S(1)}, bf16[160,2048]{1,0:T(8,128)(2,1)}, u32[]{:S(2)}, u32[]{:S(2)}) collective-permute-start(bf16[160,2048]{1,0:T(8,128)(2,1)S(1)} %param.9), channel_id=1, source_target_pairs={{0,160},{16,176},{32,128},{48,144},{64,224},{80,240},{96,192},{112... | collective-permute-start | bytes 1966088 | tf_op jit(solution)/shard_map/cond/branch_9_fun/ppermute | solution.py:148
  15.1 57.0 %collective-permute-done.9 = bf16[160,2048]{1,0:T(8,128)(2,1)} collective-permute-done((bf16[160,2048]{1,0:T(8,128)(2,1)S(1)}, bf16[160,2048]{1,0:T(8,128)(2,1)}, u32[]{:S(2)}, u32[]{:S(2)}) %collective-permute-start.9) | collective-permute-done | bytes 655392 | tf_op jit(solution)/shard_map/cond/branch_9_fun/ppermute | solution.py:148
  72.1 0.9 copy.5
  73.0 1.0 reshape.54.rec_ref
  74.0 0.2 negate_multiply_fusion
  74.2 23.8 %correlate.1 = bf16[160,320]{1,0:T(8,128)(2,1)S(1)} custom-call(bf16[160,2048]{1,0:T(8,128)(2,1)} %get-tuple-element.133.src_ref, bf16[320,2048]{1,0:T(8,128)(2,1)S(1)} %reshape.54.rec_ref, f32[16,512]{1,0:T(8,128)S(1)} %get-tuple-element.132.cos_ref, f32[16,512]{1,0:T(8,128)S(1)} %get-tuple-element.131.sin_ref), custom_call_target="tpu_custom_call" | custom-call | flops 3355443200 | bytes 2621440 | tf_op jit(solution)/shard_map/correlate/pallas_call | solution.py:121
  98.1 12.6 %conditional.3 = (bf16[160,320]{1,0:T(8,128)(2,1)}) conditional(s32[]{:T(128)} %bitcast, bf16[160,320]{1,0:T(8,128)(2,1)S(1)} %correlate.1, bf16[160,320]{1,0:T(8,128)(2,1)S(1)} %correlate.1, bf16[160,320]{1,0:T(8,128)(2,1)S(1)} %correlate.1, bf16[160,320]{1,0:T(8,128)(2,1)S(1)} %correlate.1, ...), branch_computations={%region_32.0_spmd, %region_33.0_spmd, %region_34.0_spmd, %region_3... | conditional | bytes 409648 | solution.py:148
  98.1 1.9 %collective-permute-start.40 = (bf16[160,320]{1,0:T(8,128)(2,1)S(1)}, bf16[160,320]{1,0:T(8,128)(2,1)}, u32[]{:S(2)}, u32[]{:S(2)}) collective-permute-start(bf16[160,320]{1,0:T(8,128)(2,1)S(1)} %param.40), channel_id=1, source_target_pairs={{0,160},{16,176},{32,128},{48,144},{64,224},{80,240},{96,192},{112... | collective-permute-start | bytes 307208 | tf_op jit(solution)/shard_map/cond/branch_9_fun/ppermute | solution.py:148
  100.0 10.6 %collective-permute-done.40 = bf16[160,320]{1,0:T(8,128)(2,1)} collective-permute-done((bf16[160,320]{1,0:T(8,128)(2,1)S(1)}, bf16[160,320]{1,0:T(8,128)(2,1)}, u32[]{:S(2)}, u32[]{:S(2)}) %collective-permute-start.40) | collective-permute-done | bytes 102432 | tf_op jit(solution)/shard_map/cond/branch_9_fun/ppermute | solution.py:148
  110.6 1.6 %convert_bitcast_fusion = f32[1,1,16,10,320]{4,2,3,1,0:T(8,128)} fusion(bf16[10,16,320]{2,1,0:T(8,128)(2,1)} %bitcast.6), kind=kLoop, calls=%fused_computation.6 | loop fusion | flops 51200 | bytes 307200 | tf_op jit(solution)/shard_map/broadcast_in_dim | solution.py:161
  (5 shorter events, 0.1 us)
Async XLA Ops:
  0.0 4.2 %copy-start = (bf16[2,320,2,512]{3,2,1,0:T(2,128)(2,1)S(1)}, bf16[2,320,2,512]{3,2,1,0:T(2,128)(2,1)}, u32[]{:S(2)}) copy-start(bf16[2,320,2,512]{3,2,1,0:T(2,128)(2,1)} %param.65) | copy-start | bytes 3932164
  6.3 1.0 copy-start.1
  7.4 64.7 %collective-permute-start.9 = (bf16[160,2048]{1,0:T(8,128)(2,1)S(1)}, bf16[160,2048]{1,0:T(8,128)(2,1)}, u32[]{:S(2)}, u32[]{:S(2)}) collective-permute-start(bf16[160,2048]{1,0:T(8,128)(2,1)S(1)} %param.9), channel_id=1, source_target_pairs={{0,160},{16,176},{32,128},{48,144},{64,224},{80,240},{96,192},{112... | collective-permute-start | bytes 1966088 | tf_op jit(solution)/shard_map/cond/branch_9_fun/ppermute | solution.py:148
  98.1 12.5 %collective-permute-start.40 = (bf16[160,320]{1,0:T(8,128)(2,1)S(1)}, bf16[160,320]{1,0:T(8,128)(2,1)}, u32[]{:S(2)}, u32[]{:S(2)}) collective-permute-start(bf16[160,320]{1,0:T(8,128)(2,1)S(1)} %param.40), channel_id=1, source_target_pairs={{0,160},{16,176},{32,128},{48,144},{64,224},{80,240},{96,192},{112... | collective-permute-start | bytes 307208 | tf_op jit(solution)/shard_map/cond/branch_9_fun/ppermute | solution.py:148

commit v2 on v1

--- a/solution.py
+++ b/solution.py
@@ -140,7 +140,50 @@
     )(sources, receivers, cos, sin)
 
 
+def flip(index, mask):
+    for bit in range(mask.bit_length()):
+        if (mask >> bit) & 1:
+            index = index + (1 - 2 * lax.rem(index // (1 << bit), 2)) * (1 << bit)
+    return index
+
+
+def swap_kernel(mask, rows, src_ref, dst_ref, sem_s, sem_r):
+    target = (flip(lax.axis_index("chan"), mask), lax.axis_index("win"))
+    barrier = pltpu.get_barrier_semaphore()
+    pl.semaphore_signal(barrier, inc=1, device_id=target, device_id_type=MESH)
+    pl.semaphore_wait(barrier, 1)
+    copies = [
+        pltpu.make_async_remote_copy(
+            src_ref=src_ref.at[pl.ds(n * rows, rows)], dst_ref=dst_ref.at[pl.ds(n * rows, rows)],
+            send_sem=sem_s.at[n], recv_sem=sem_r.at[n], device_id=target, device_id_type=MESH,
+        )
+        for n in range(src_ref.shape[0] // rows)
+    ]
+    for copy in copies:
+        copy.start()
+    for copy in copies:
+        copy.wait()
+
+
+def swap(mask, rows, values):
+    parts = values.shape[0] // rows
+    return pl.pallas_call(
+        functools.partial(swap_kernel, mask, rows),
+        out_shape=jax.ShapeDtypeStruct(values.shape, values.dtype),
+        in_specs=[pl.BlockSpec(memory_space=pl.ANY)],
+        out_specs=pl.BlockSpec(memory_space=pl.ANY),
+        scratch_shapes=[pltpu.SemaphoreType.DMA((parts,)), pltpu.SemaphoreType.DMA((parts,))],
+        compiler_params=pltpu.CompilerParams(collective_id=mask, has_side_effects=True),
+        name="swap",
+    )(values)
+
+
 def exchange(values, flags, size):
+    branches = [functools.partial(swap, t, 32) for t in range(1, size)]
+    return lax.switch(flags - 1, branches, values)
+
+
+def send_back(values, flags, size):
     branches = [
         functools.partial(lax.ppermute, axis_name="chan", perm=[(i, i ^ t) for i in range(size)])
         for t in range(1, size)
@@ -156,7 +199,7 @@
     flags = partner[0, 0]
     sources = exchange(white[:SRC], flags, size)
     block = correlate(sources, white, cos, sin, 1.0 / math.sqrt(windows))
-    block = exchange(block, flags, size)
+    block = send_back(block, flags, size)
     out = jnp.swapaxes(block.astype(jnp.float32).reshape(SRC // 16, LAGS, white.shape[0]), 0, 1)
     return out[None, None]
 

time: 112 us -> 130 us (1.16)
  Pallas kernels: 23.8 us -> 105 us
  waiting for transfers between devices: 67.5 us -> 10.6 us
  starting transfers between devices: 9.67 us -> 1.92 us
    pallas_call x0 -> x1, Pallas kernels: none -> 82.4 us  [swap(): pl.pallas_call(functools.partial(swap_kernel, mask, rows), out_shape=jax....]
    ppermute x2 -> x1, waiting for transfers between devices: 67.5 us -> 10.6 us  [send_back(): return lax.switch(flags - 1, branches, values)]
    ppermute x2 -> x1, starting transfers between devices: 9.67 us -> 1.92 us  [send_back(): return lax.switch(flags - 1, branches, values)]
  transfers between devices with their start and end apart: 2 -> 1, of which waited for: 2 -> 1; matrix products, arithmetic and copies ran while one was open for 0% -> 0% of each run, Pallas kernels for 0% -> 0%
where the time goes in v2:
time: 130 us
  Pallas kernels  105 us (81%)
  waiting for transfers between devices  10.6 us (8%)
  other arithmetic  7.02 us (5%)
  local copies, waits for them, and re-layouts  4.14 us (3%)
  starting transfers between devices  1.92 us (1%)
    pallas_call x1, Pallas kernels, swap(): pl.pallas_call(functools.partial(swap_kernel, mask, rows), out_shape=jax....  82.4 us
    pallas_call x1, Pallas kernels, correlate(): pl.pallas_call(functools.partial(correlate_kernel, scale), out_shape=jax....  23.1 us
    ppermute x1, waiting for transfers between devices, send_back(): return lax.switch(flags - 1, branches, values)  10.6 us
    reduce_sum x1, other arithmetic, whiten_rows(): power = jnp.mean(values * values, axis=(2, 3))  3.49 us
  transfers between devices with their start and end apart: 1, of which 1 were waited for; matrix products, arithmetic and copies ran while one was open for 0% of the time, Pallas kernels for 0%

profile of v2, /device:TPU:34, one launch (start us, length us, event | category | flops | bytes accessed | tf_op | source)
XLA Modules:
  0.0 130.1 jit_solution(13584732662158901951)
XLA Ops:
  0.0 0.0 copy-start
  0.0 3.5 %fusion.2 = f32[2,320]{1,0:T(2,128)S(1)} fusion(bf16[2,320,2,512]{3,2,1,0:T(2,128)(2,1)} %param.65), kind=kLoop, calls=%fused_computation.4 | loop fusion | flops 1965440 | bytes 1313280 | tf_op jit(solution)/shard_map/reduce_sum | solution.py:22
  4.2 0.0 copy-done
  4.2 1.6 %fusion.3 = bf16[320,2,2,512]{3,2,0,1:T(2,128)(2,1)S(1)} fusion(bf16[2,320,2,512]{3,2,1,0:T(2,128)(2,1)S(1)} %copy-done, f32[2,320]{1,0:T(2,128)S(1)} %rsqrt_multiply_fusion, f32[512]{0:T(512)S(1)} %multiply_subtract_fusion), kind=kLoop, calls=%fused_computation.5 | loop fusion | flops 2621440 | bytes 2626048 | tf_op jit(solution)/shard_map/transpose | solution.py:25
  5.9 0.5 slice.105
  6.3 0.0 copy-start.3
  6.3 0.5 copy.4
  6.8 0.5 slice.104
  7.3 0.0 copy-done.3
  7.4 82.4 %conditional.2 = (bf16[160,2048]{1,0:T(8,128)(2,1)S(1)}) conditional(s32[]{:T(128)} %bitcast, bf16[160,2048]{1,0:T(8,128)(2,1)S(1)} %slice.104, bf16[160,2048]{1,0:T(8,128)(2,1)S(1)} %slice.104, bf16[160,2048]{1,0:T(8,128)(2,1)S(1)} %slice.104, bf16[160,2048]{1,0:T(8,128)(2,1)S(1)} %slice.104, ...), branch_computations={%region_1.0_spmd, %region_2.0_spmd, %region_3.0_spmd, %region_4.0_... | conditional | bytes 8 | solution.py:183
  7.4 82.4 %swap.40 = bf16[160,2048]{1,0:T(8,128)(2,1)S(1)} custom-call(bf16[160,2048]{1,0:T(8,128)(2,1)S(1)} %src_ref.9), custom_call_target="tpu_custom_call" | custom-call | tf_op jit(solution)/shard_map/cond/branch_9_fun/swap/pallas_call | solution.py:170
  89.8 0.0 copy-start.1
  89.8 0.8 copy-done.1
  90.6 0.9 copy.5
  91.5 0.0 copy-start.2
  91.5 1.0 reshape.54.rec_ref
  92.6 0.2 negate_multiply_fusion
  92.8 0.0 copy-done.2
  92.8 23.1 %correlate.1 = bf16[160,320]{1,0:T(8,128)(2,1)S(1)} custom-call(bf16[160,2048]{1,0:T(8,128)(2,1)S(1)} %copy-done.2, bf16[320,2048]{1,0:T(8,128)(2,1)S(1)} %reshape.54.rec_ref, f32[16,512]{1,0:T(8,128)S(1)} %get-tuple-element.132.cos_ref, f32[16,512]{1,0:T(8,128)S(1)} %get-tuple-element.131.sin_ref), custom_call_target="tpu_custom_call" | custom-call | flops 3355443200 | bytes 2621440 | tf_op jit(solution)/shard_map/correlate/pallas_call | solution.py:121
  115.9 12.6 %conditional.3 = (bf16[160,320]{1,0:T(8,128)(2,1)}) conditional(s32[]{:T(128)} %bitcast, bf16[160,320]{1,0:T(8,128)(2,1)S(1)} %correlate.1, bf16[160,320]{1,0:T(8,128)(2,1)S(1)} %correlate.1, bf16[160,320]{1,0:T(8,128)(2,1)S(1)} %correlate.1, bf16[160,320]{1,0:T(8,128)(2,1)S(1)} %correlate.1, ...), branch_computations={%region_32.0_spmd, %region_33.0_spmd, %region_34.0_spmd, %region_3... | conditional | bytes 409648 | solution.py:191
  115.9 1.9 %collective-permute-start.9 = (bf16[160,320]{1,0:T(8,128)(2,1)S(1)}, bf16[160,320]{1,0:T(8,128)(2,1)}, u32[]{:S(2)}, u32[]{:S(2)}) collective-permute-start(bf16[160,320]{1,0:T(8,128)(2,1)S(1)} %param.40), channel_id=1, source_target_pairs={{0,160},{16,176},{32,128},{48,144},{64,224},{80,240},{96,192},{112... | collective-permute-start | bytes 307208 | tf_op jit(solution)/shard_map/cond/branch_9_fun/ppermute | solution.py:191
  117.9 10.6 %collective-permute-done.9 = bf16[160,320]{1,0:T(8,128)(2,1)} collective-permute-done((bf16[160,320]{1,0:T(8,128)(2,1)S(1)}, bf16[160,320]{1,0:T(8,128)(2,1)}, u32[]{:S(2)}, u32[]{:S(2)}) %collective-permute-start.9) | collective-permute-done | bytes 102432 | tf_op jit(solution)/shard_map/cond/branch_9_fun/ppermute | solution.py:191
  128.4 1.6 %convert_bitcast_fusion = f32[1,1,16,10,320]{4,2,3,1,0:T(8,128)} fusion(bf16[10,16,320]{2,1,0:T(8,128)(2,1)} %bitcast.6), kind=kLoop, calls=%fused_computation.6 | loop fusion | flops 51200 | bytes 307200 | tf_op jit(solution)/shard_map/broadcast_in_dim | solution.py:204
  (5 shorter events, 0.1 us)
Async XLA Ops:
  0.0 4.2 %copy-start = (bf16[2,320,2,512]{3,2,1,0:T(2,128)(2,1)S(1)}, bf16[2,320,2,512]{3,2,1,0:T(2,128)(2,1)}, u32[]{:S(2)}) copy-start(bf16[2,320,2,512]{3,2,1,0:T(2,128)(2,1)} %param.65) | copy-start | bytes 3932164
  6.3 1.0 copy-start.3
  89.8 0.8 copy-start.1
  91.5 1.2 copy-start.2
  115.9 12.5 %collective-permute-start.9 = (bf16[160,320]{1,0:T(8,128)(2,1)S(1)}, bf16[160,320]{1,0:T(8,128)(2,1)}, u32[]{:S(2)}, u32[]{:S(2)}) collective-permute-start(bf16[160,320]{1,0:T(8,128)(2,1)S(1)} %param.40), channel_id=1, source_target_pairs={{0,160},{16,176},{32,128},{48,144},{64,224},{80,240},{96,192},{112... | collective-permute-start | bytes 307208 | tf_op jit(solution)/shard_map/cond/branch_9_fun/ppermute | solution.py:191

commit v3 on v0

v3 whole, which is shorter than its diff:
```python
import functools
import math

import jax
import jax.numpy as jnp
import numpy as np
from jax import lax
from jax.experimental import pallas as pl
from jax.experimental.pallas import tpu as pltpu
from jax.sharding import PartitionSpec as P

LAGS = 16
SRC = 160
WIN = 16
PER = SRC // WIN
GROUP = 1
UNITS = PER // GROUP
STRIP = 32
DEPTH = 256
AHEAD = 3
MESH = pl.DeviceIdType.MESH


def lag_table(freqs):
    freq = np.arange(freqs, dtype=np.float64) + freqs // 4
    delay = np.arange(LAGS, dtype=np.float64) - LAGS // 2
    phase = 2.0 * np.pi * freq[None, :] * delay[:, None] / (4.0 * freqs)
    norm = 1.0 / math.sqrt(2.0 * freqs)
    return np.float32(np.cos(phase) * norm), np.float32(-np.sin(phase) * norm)


def taper_row(freqs):
    freq = np.arange(freqs, dtype=np.float64)
    taper = 0.75 - 0.25 * np.cos(2.0 * np.pi * (freq + 0.5) / freqs)
    return np.float32(np.concatenate([taper, taper])[None])


def flip(index, mask):
    for bit in range(mask.bit_length()):
        if (mask >> bit) & 1:
            index = index + (1 - 2 * lax.rem(index // (1 << bit), 2)) * (1 << bit)
    return index


def kernel(
    mask, scale, raw_ref, count_ref, taper_ref, cos_ref, sin_ref, out_ref,
    white, mine, theirs, rec_t, unit32, mixed, sums, part, own, send1, recv1, send2, recv2, back, landed,
    sem_xs, sem_xr, sem_1s, sem_1r, sem_2s, sem_2r, sem_bs, sem_br,
):
    chan, win = lax.axis_index("chan"), lax.axis_index("win")
    y, x, core = win // 8, lax.rem(win // 2, 4), lax.rem(win, 2)
    sibling = win + 1 - 2 * core
    partner = flip(chan, mask)
    freqs = cos_ref.shape[1]
    width = 2 * freqs
    count, total_width = raw_ref.shape
    wins = total_width // width
    rows = GROUP * LAGS

    def place(d):
        return lax.rem(y + d // 4, 2) * 8 + lax.rem(x + lax.rem(d, 4), 4) * 2

    barrier = pltpu.get_barrier_semaphore()
    pl.semaphore_signal(barrier, inc=1, device_id=(partner, win), device_id_type=MESH)
    pl.semaphore_signal(barrier, inc=1, device_id=(chan, sibling), device_id_type=MESH)

    @pl.loop(1, 8)
    def _(d):
        pl.semaphore_signal(barrier, inc=1, device_id=(chan, place(d) + core), device_id_type=MESH)

    def copy_x(unit):
        return pltpu.make_async_remote_copy(
            src_ref=mine.at[unit], dst_ref=theirs.at[unit], send_sem=sem_xs.at[unit], recv_sem=sem_xr.at[unit],
            device_id=(partner, win), device_id_type=MESH,
        )

    def copy_1(unit):
        return pltpu.make_async_remote_copy(
            src_ref=send1.at[unit], dst_ref=recv1.at[unit], send_sem=sem_1s.at[unit], recv_sem=sem_1r.at[unit],
            device_id=(chan, sibling), device_id_type=MESH,
        )

    def copy_2(unit, d, count=1):
        return pltpu.make_async_remote_copy(
            src_ref=send2.at[unit, pl.ds(d, count)], dst_ref=recv2.at[unit, pl.ds(d, count)],
            send_sem=sem_2s.at[unit], recv_sem=sem_2r.at[unit],
            device_id=(chan, place(d) + core), device_id_type=MESH,
        )

    def copy_b(unit):
        return pltpu.make_async_remote_copy(
            src_ref=back.at[unit], dst_ref=landed.at[unit], send_sem=sem_bs.at[unit], recv_sem=sem_br.at[unit],
            device_id=(partner, win), device_id_type=MESH,
        )

    def whiten(first, last):
        @pl.loop(first // STRIP, last // STRIP)
        def _(strip):
            at = pl.ds(pl.multiple_of(strip * STRIP, STRIP), STRIP)
            channel = strip * STRIP + lax.broadcasted_iota(jnp.int32, (STRIP, 1), 0)
            valid = jnp.where(channel < count_ref[...], 1.0, 0.0)
            for w in range(wins):
                piece = slice(w * width, (w + 1) * width)
                values = raw_ref[at, piece].astype(jnp.float32)
                power = jnp.sum(values * values, axis=1, keepdims=True) * (1.0 / width)
                values = values * taper_ref[...] * (valid / jnp.sqrt(power + 1e-05))
                for n in range(width // 128):
                    white[w * (width // 128) + n, at, :] = values[:, n * 128 : (n + 1) * 128]

    whiten(0, SRC)
    pl.semaphore_wait(barrier, 9)

    @pl.loop(0, UNITS)
    def _(unit):
        for i in range(GROUP):
            for n in range(total_width // 128):
                chosen = white[n, pl.ds(unit * GROUP + i, WIN, stride=PER), :]
                mine[unit, i * WIN : (i + 1) * WIN, n * 128 : (n + 1) * 128] = chosen.astype(jnp.bfloat16)

        @pl.when(unit < AHEAD)
        def _():
            copy_x(unit).start()

    whiten(SRC, count)

    @pl.loop(0, total_width // 128)
    def _(n):
        at = pl.ds(pl.multiple_of(n * 128, 128), 128)
        rec_t[at, :] = white[n].T.astype(jnp.bfloat16)

    def terms(unit):
        copy_x(unit).wait_recv()

        @pl.when(unit < UNITS - AHEAD)
        def _():
            copy_x(unit + AHEAD).start()

        unit32[...] = theirs[unit].astype(jnp.float32)

        @pl.loop(0, 16)
        def _(n):
            dest = place(lax.rem(n, 8)) + jnp.where(n < 8, 1 - core, core)
            cos, sin = cos_ref[...], sin_ref[...]
            for i in range(GROUP):
                source = i * WIN + dest
                into = pl.ds(pl.multiple_of(n * rows + i * LAGS, LAGS), LAGS)
                for w in range(wins):
                    a, b, c = w * width, w * width + freqs, (w + 1) * width
                    first, second = unit32[pl.ds(source, 1), a:b], unit32[pl.ds(source, 1), b:c]
                    mixed[into, a:b] = (first * cos + second * sin).astype(jnp.bfloat16)
                    mixed[into, b:c] = (second * cos - first * sin).astype(jnp.bfloat16)

        sums[...] = jnp.zeros_like(sums)

        @pl.loop(0, total_width // DEPTH)
        def _(n):
            at = pl.ds(pl.multiple_of(n * DEPTH, DEPTH), DEPTH)
            sums[...] += jnp.dot(mixed[:, at], rec_t[at, :], preferred_element_type=jnp.float32)

        send1[unit] = sums[: 8 * rows].astype(jnp.bfloat16).reshape(8, rows, count)
        copy_1(unit).start()
        part[lax.rem(unit, 2)] = sums[8 * rows :].reshape(8, rows, count)

    def pair_sums(unit):
        copy_1(unit).wait_recv()
        total = part[lax.rem(unit, 2)] + recv1[unit].astype(jnp.float32)
        own[lax.rem(unit, 2)] = total[0]
        send2[unit] = total.astype(jnp.bfloat16)

        @pl.loop(1, 8)
        def _(d):
            copy_2(unit, d).start()

    def all_sums(unit):
        copy_2(unit, 1, 7).wait_recv()
        total = own[lax.rem(unit, 2)]
        for d in range(1, 8):
            total = total + recv2[unit, d].astype(jnp.float32)
        back[unit] = (total * scale).astype(jnp.bfloat16)
        copy_b(unit).start()

    @pl.loop(0, UNITS + 2)
    def _(unit):
        @pl.when(unit < UNITS)
        def _():
            terms(unit)

        @pl.when((unit >= 1) & (unit < UNITS + 1))
        def _():
            pair_sums(unit - 1)

        @pl.when(unit >= 2)
        def _():
            all_sums(unit - 2)

    @pl.loop(0, UNITS)
    def _(unit):
        copy_x(unit).wait_send()
        copy_1(unit).wait_send()
        copy_2(unit, 1, 7).wait_send()
        copy_b(unit).wait_send()
        copy_b(unit).wait_recv()
        out_ref[unit] = landed[unit]


def correlate(mask, scale, raw, count, taper, cos, sin):
    channels, width = raw.shape
    rows = GROUP * LAGS
    blocks = pltpu.VMEM((UNITS, 8, rows, channels), jnp.bfloat16)
    units = pltpu.VMEM((UNITS, WIN * GROUP, width), jnp.bfloat16)
    results = pltpu.VMEM((UNITS, rows, channels), jnp.bfloat16)
    whole = pl.BlockSpec(memory_space=pltpu.VMEM)
    each = pltpu.SemaphoreType.DMA((UNITS,))
    return pl.pallas_call(
        functools.partial(kernel, mask, scale),
        out_shape=jax.ShapeDtypeStruct((UNITS, rows, channels), jnp.bfloat16),
        in_specs=[whole] * 5,
        out_specs=whole,
        scratch_shapes=[
            pltpu.VMEM((width // 128, channels, 128), jnp.float32),
            units, units,
            pltpu.VMEM((width, channels), jnp.bfloat16),
            pltpu.VMEM((WIN * GROUP, width), jnp.float32),
            pltpu.VMEM((16 * rows, width), jnp.bfloat16),
            pltpu.VMEM((16 * rows, channels), jnp.float32),
            pltpu.VMEM((2, 8, rows, channels), jnp.float32),
            pltpu.VMEM((2, rows, channels), jnp.float32),
            blocks, blocks, blocks, blocks, results, results,
            each, each, each, each, each, each, each, each,
        ],
        compiler_params=pltpu.CompilerParams(
            collective_id=mask, has_side_effects=True, vmem_limit_bytes=32 * 1024 * 1024
        ),
        cost_estimate=pl.CostEstimate(
            flops=2 * SRC * LAGS * channels * width, bytes_accessed=4 * channels * width, transcendentals=0
        ),
        name="correlate",
    )(raw, count, taper, cos, sin)


def body(spectra, counts, partner):
    wins, channels, two, freqs = spectra.shape
    size = lax.axis_size("chan")
    scale = 1.0 / math.sqrt(wins * lax.axis_size("win"))
    raw = jnp.swapaxes(spectra, 0, 1).reshape(channels, wins * two * freqs)
    operands = (raw, counts.reshape(1, 1), taper_row(freqs), *lag_table(freqs))
    branches = [functools.partial(correlate, t, scale) for t in range(1, size)]
    block = lax.switch(partner[0, 0] - 1, branches, *operands)
    out = block.reshape(PER, LAGS, channels).astype(jnp.float32)
    return jnp.swapaxes(out, 0, 1)[None, None]


def solution(mesh):
    return jax.shard_map(
        body,
        mesh=mesh,
        in_specs=(P("win", "chan", None, None), P("chan"), P()),
        out_specs=P("chan", None, None, "win", None),
        check_vma=False,
    )
```

time: 575 us -> 112 us (0.19)
  the two profiles are of different devices: /device:TPU:32 before, /device:TPU:1 now
where the time goes in v3:
time: 112 us; the launch traced here: 111 us
  Pallas kernels  107 us (96%)
  local copies, waits for them, and re-layouts  3.24 us (3%)
    pallas_call x1, Pallas kernels, correlate(): pl.pallas_call(functools.partial(kernel, mask, scale), out_shape=jax.Shap...  107 us

profile of v3, /device:TPU:1, one launch (start us, length us, event | category | flops | bytes accessed | tf_op | source)
XLA Modules:
  0.0 111.4 jit_solution(17768560068382834744)
XLA Ops:
  0.0 2.2 %copy.7 = bf16[320,2,2,512]{3,2,1,0:T(2,128)(2,1)S(1)} copy(bf16[320,2,2,512]{3,2,0,1:T(2,128)(2,1)} %bitcast.8) | data formatting | bytes 2621440 | tf_op jit(solution)/shard_map/transpose | solution.py:245
  2.2 0.0 copy-start
  2.2 0.0 copy-start.1
  2.2 0.0 copy-start.2
  2.3 0.0 copy-start.3
  2.3 1.0 reshape.11
  3.3 0.0 copy-done
  3.3 0.0 copy-done.1
  3.3 0.0 copy-done.2
  3.3 0.0 copy-done.3
  3.4 107.3 %conditional.1 = (bf16[10,16,320]{2,1,0:T(8,128)(2,1)S(1)}) conditional(s32[]{:T(128)} %bitcast, (bf16[320,2048]{1,0:T(8,128)(2,1)S(1)}, s32[1,1]{1,0:T(1,128)}, f32[1,1024]{1,0:T(1,128)S(1)}, f32[16,512]{1,0:T(8,128)S(1)}, f32[16,512]{1,0:T(8,128)S(1)}) %tuple.192, (bf16[320,2048]{1,0:T(8,128)(2,1)S(1)}, ...), branch_computations={%region_0.0_spmd, %region_1.0_spmd, %region_2.0_spmd, %region_3.0_... | conditional | flops 3355443200 | bytes 2621448 | solution.py:248
  3.6 107.1 %correlate.55 = bf16[10,16,320]{2,1,0:T(8,128)(2,1)S(1)} custom-call(bf16[320,2048]{1,0:T(8,128)(2,1)S(1)} %get-tuple-element.467.raw_ref, s32[1,1]{1,0:T(1,128)} %get-tuple-element.468.count_ref, f32[1,1024]{1,0:T(1,128)S(1)} %get-tuple-element.469.taper_ref, f32[16,512]{1,0:T(8,128)S(1)} %get-tuple-element.470.cos_ref, ...), custom_call_target="tpu_custom_call" | custom-call | flops 3355443200 | bytes 2621440 | tf_op jit(solution)/shard_map/cond/branch_24_fun/correlate/pallas_call | solution.py:214
  110.7 0.7 convert_bitcast_fusion
Async XLA Ops:
  2.2 1.1 copy-start
  2.2 1.1 copy-start.1
  2.2 1.1 copy-start.2
  2.3 1.1 copy-start.3
